TPU v7x, 32 devices: a whole 2x2x4 slice. The times are simulated.
32 devices in a mesh: layer: 4 (over y, core), blk: 8 (over z, x).
Axes of the slice: x: 2, y: 2, z: 4, core: 2. Of those that a mesh axis runs over, the one named last changes fastest.
Arguments:
- source: bfloat16 [4, 2, 128, 32768], P('layer', None, None, 'blk'), may hold values from -6 to 6
- tile_data: bfloat16 [4, 192, 2, 512, 512], P('layer', 'blk'), may hold values from -0.078125 to 0.078125
- tile_rows: int32 [4, 192], P('layer', 'blk'), may hold values from 0 to 63, as said below
- tile_cols: int32 [4, 192], P('layer', 'blk'), may hold values from 0 to 63, as said below
- tile_count: int32 [4, 8], P('layer', 'blk'), may hold values from 10 to 24, as said below
Outputs:
- down_trace: bfloat16 [4, 2, 128, 32768], P('layer', None, None, 'blk')
- up_trace: bfloat16 [4, 2, 128, 32768], P('layer', None, None, 'blk')
Inputs may be any that keep to these rules, and one draw needn't show every extreme that they name: `tile_rows`: every slot of row range g (slots g*24 to (g+1)*24 - 1) has its row block in g*8 to (g+1)*8 - 1; the live slots of one range hold distinct tiles in shuffled order, among them the diagonal tile of each of its row blocks, and the tile one block left of its first row block and one block right of its last where those exist. Slots that are not live also hold valid indices. `tile_cols`: every slot's column block lies within 2 blocks of its row block, inside the grid. `tile_count`: in every section some row range has all 24 slots live.
All inputs are finite; a program needn't handle non-finite values.
Results may differ from a plain program's by a relative error of at most 0.01.
Values may be sent and summed in bfloat16 or wider, within the bound.
A program may use at most 64 MiB of HBM per device.

v0:
```python
import jax
import jax.numpy as jnp
from jax import lax
from jax.sharding import PartitionSpec as P

BATCHES = 2
BAND = 2


def padded(shard, sides, width):
    for axis, dim in sides:
        devices, length = (lax.axis_size(axis), shard.shape[dim])
        up = [(i, (i + 1) % devices) for i in range(devices - 1)]
        down = [(j, i) for i, j in up]
        last = lax.slice_in_dim(shard, length - width, length, axis=dim)
        initial = lax.slice_in_dim(shard, 0, width, axis=dim)
        before = lax.ppermute(last, axis, up)
        after = lax.ppermute(initial, axis, down)
        shard = jnp.concatenate([before, shard, after], axis=dim)
    return shard


def from_behind(block, axis, distance):
    devices = range(lax.axis_size(axis))
    route = [(i - distance, i) for i in devices if i - distance in devices]
    return lax.ppermute(block, axis, route)


def complex_apply(segment, matrix, contract):
    halves = segment.shape[1]
    flattened = segment.reshape(2 * halves, segment.shape[2])
    numbers = (((1,), (contract,)), ((), ()))
    with_real = lax.dot_general(flattened, matrix[0], numbers, preferred_element_type=jnp.float32)
    with_imag = lax.dot_general(flattened, matrix[1], numbers, preferred_element_type=jnp.float32)
    return jnp.stack(
        (with_real[:halves] - with_imag[halves:], with_imag[:halves] + with_real[halves:])
    )


def on_device(source, tile_data, tile_rows, tile_cols, tile_count):
    layers = lax.axis_size("layer")
    layer_index = lax.axis_index("layer")
    tile_size = tile_data.shape[3]
    rows_dev = source.shape[3]
    all_columns = source.shape[2]
    margin = BAND * tile_size
    first_block = lax.axis_index("blk") * (rows_dev // tile_size)
    batch_count = BATCHES
    columns = all_columns // batch_count
    live_count = tile_count[0, 0]
    row_start = (tile_rows[0] - first_block) * tile_size
    col_start = (tile_cols[0] - first_block) * tile_size + margin
    local_tiles = tile_data[0]
    sources = source[0]
    part_shape = (2, columns, rows_dev)
    step_count = layers + batch_count - 1

    def down_step(step_index, state_pair):
        incoming, collected = state_pair
        batch_index = step_index - layer_index
        active = (batch_index >= 0) & (batch_index < batch_count)
        offset = jnp.clip(batch_index, 0, batch_count - 1) * columns
        present = lax.dynamic_slice_in_dim(sources, offset, columns, 1)
        current = (present.astype(jnp.float32) + incoming.astype(jnp.float32)).astype(jnp.bfloat16)
        earlier = lax.dynamic_slice_in_dim(collected, offset, columns, 1)
        collected = lax.dynamic_update_slice_in_dim(
            collected, jnp.where(active, current, earlier), offset, 1
        )
        extended = padded(current, (("blk", 2),), margin)

        def down_add_tile(slot_index, summed):
            segment = lax.dynamic_slice_in_dim(extended, col_start[slot_index], tile_size, 2)
            matrix = lax.dynamic_index_in_dim(local_tiles, slot_index, 0, keepdims=False)
            product = complex_apply(segment, matrix, 1)
            target = lax.dynamic_slice_in_dim(summed, row_start[slot_index], tile_size, 2)
            return lax.dynamic_update_slice_in_dim(
                summed, target + product, row_start[slot_index], 2
            )

        forward = lax.fori_loop(
            0, jnp.where(active, live_count, 0), down_add_tile, jnp.zeros(part_shape, jnp.float32)
        )
        incoming = from_behind(forward.astype(jnp.bfloat16), "layer", 1)
        return (incoming, collected)

    empty_part = jnp.zeros(part_shape, jnp.bfloat16)
    down_trace = lax.fori_loop(0, step_count, down_step, (empty_part, jnp.zeros_like(sources)))[1]

    def up_step(step_index, state_pair):
        incoming, collected = state_pair
        batch_index = step_index - (layers - 1 - layer_index)
        active = (batch_index >= 0) & (batch_index < batch_count)
        offset = jnp.clip(batch_index, 0, batch_count - 1) * columns
        present = lax.dynamic_slice_in_dim(down_trace, offset, columns, 1)
        current = (present.astype(jnp.float32) + incoming.astype(jnp.float32)).astype(jnp.bfloat16)
        earlier = lax.dynamic_slice_in_dim(collected, offset, columns, 1)
        collected = lax.dynamic_update_slice_in_dim(
            collected, jnp.where(active, current, earlier), offset, 1
        )

        def up_add_tile(slot_index, summed):
            segment = lax.dynamic_slice_in_dim(current, row_start[slot_index], tile_size, 2)
            matrix = lax.dynamic_index_in_dim(local_tiles, slot_index, 0, keepdims=False)
            product = complex_apply(segment, matrix, 0)
            target = lax.dynamic_slice_in_dim(summed, col_start[slot_index], tile_size, 2)
            return lax.dynamic_update_slice_in_dim(
                summed, target + product, col_start[slot_index], 2
            )

        extended = lax.fori_loop(
            0,
            jnp.where(active, live_count, 0),
            up_add_tile,
            jnp.zeros((2, columns, rows_dev + 2 * margin), jnp.float32),
        )
        lower_rim = extended[:, :, :margin].astype(jnp.bfloat16)
        upper_rim = extended[:, :, margin + rows_dev :].astype(jnp.bfloat16)
        from_above = from_behind(lower_rim, "blk", -1)
        from_below = from_behind(upper_rim, "blk", 1)
        backward = extended[:, :, margin : margin + rows_dev]
        backward = backward + jnp.pad(
            from_below.astype(jnp.float32), ((0, 0), (0, 0), (0, rows_dev - margin))
        )
        backward = backward + jnp.pad(
            from_above.astype(jnp.float32), ((0, 0), (0, 0), (rows_dev - margin, 0))
        )
        incoming = from_behind(backward.astype(jnp.bfloat16), "layer", -1)
        return (incoming, collected)

    up_trace = lax.fori_loop(0, step_count, up_step, (empty_part, jnp.zeros_like(sources)))[1]
    return (down_trace[None], up_trace[None])


def solution(mesh):
    in_specs = (
        P("layer", None, None, "blk"),
        P("layer", "blk", None, None, None),
        P("layer", "blk"),
        P("layer", "blk"),
        P("layer", "blk"),
    )
    out_specs = (P("layer", None, None, "blk"), P("layer", None, None, "blk"))
    return jax.shard_map(
        on_device, mesh=mesh, in_specs=in_specs, out_specs=out_specs, check_vma=False
    )
```

profile of v0, /device:TPU:25, one launch (start us, length us, event | category | flops | bytes accessed | tf_op | source)
XLA Modules:
  0.0 2529.4 jit_solution(14713949243050410749)
XLA Ops:
  3.0 1080.4 %while.86 = (s32[]{:T(128)}, bf16[2,64,4096]{2,1,0:T(8,128)(2,1)S(1)}, bf16[2,128,4096]{2,1,0:T(8,128)(2,1)}, s32[]{:T(128)}, s32[]{:T(128)}, /*index=5*/bf16[2,...) while((s32[]{:T(128)}, ...), condition=%wide.region_3.4_spmd, body=%wide.region_0.3_spmd.sunk | while | flops 142278672 | bytes 25166664 | solution.py:87
  3.0 3.1 select_dynamic-update-slice_fusion.4
  6.1 3.0 collective-permute-start.3
  9.2 2.3 collective-permute-start.4
  12.1 8.7 collective-permute-done.3
  23.4 4.6 collective-permute-start.5
  28.0 216.3 %collective-permute-done.5 = bf16[2,64,4096]{2,1,0:T(8,128)(2,1)S(1)} collective-permute-done((bf16[2,64,4096]{2,1,0:T(8,128)(2,1)}, bf16[2,64,4096]{2,1,0:T(8,128)(2,1)S(1)}, u32[]{:S(2)}, u32[]{:S(2)}) %collective-permute-start.5) | collective-permute-done | bytes 1048608 | tf_op jit(solution)/shard_map/while/body/eval_jaxpr/ppermute | solution.py:26
  244.3 3.1 select_dynamic-update-slice_fusion.4
  247.5 1.9 collective-permute-start.3
  249.4 3.4 collective-permute-start.4
  253.4 9.3 collective-permute-done.3
  264.2 156.9 %while.89 = (s32[]{:T(128)}, f32[2,64,4096]{2,1,0:T(8,128)S(1)}, s32[]{:T(128)}, s32[24]{0:T(128)S(1)}, s32[24]{0:T(128)S(1)}, /*index=5*/bf16[2,64,6144]{2,1,0:...) while((s32[]{:T(128)}, f32[2,64,4096]{2,1,0:T(8,128)S(1)}, ...), condition=%wide.region_2.2_spmd, body=%wide.region_1.1_spmd.sunk | while | flops 134414336 | bytes 4194599 | solution.py:80
  424.2 61.5 %collective-permute-done.5 = bf16[2,64,4096]{2,1,0:T(8,128)(2,1)S(1)} collective-permute-done((bf16[2,64,4096]{2,1,0:T(8,128)(2,1)}, bf16[2,64,4096]{2,1,0:T(8,128)(2,1)S(1)}, u32[]{:S(2)}, u32[]{:S(2)}) %collective-permute-start.5) | collective-permute-done | bytes 1048608 | tf_op jit(solution)/shard_map/while/body/eval_jaxpr/ppermute | solution.py:26
  485.7 3.1 select_dynamic-update-slice_fusion.4
  488.8 1.9 collective-permute-start.3
  490.8 3.4 collective-permute-start.4
  494.8 9.3 collective-permute-done.3
  505.6 156.9 %while.89 = (s32[]{:T(128)}, f32[2,64,4096]{2,1,0:T(8,128)S(1)}, s32[]{:T(128)}, s32[24]{0:T(128)S(1)}, s32[24]{0:T(128)S(1)}, /*index=5*/bf16[2,64,6144]{2,1,0:...) while((s32[]{:T(128)}, f32[2,64,4096]{2,1,0:T(8,128)S(1)}, ...), condition=%wide.region_2.2_spmd, body=%wide.region_1.1_spmd.sunk | while | flops 134414336 | bytes 4194599 | solution.py:80
  663.6 15.0 collective-permute-start.5
  678.6 12.0 collective-permute-done.5
  690.7 3.1 select_dynamic-update-slice_fusion.4
  693.8 91.7 %collective-permute-start.3 = (bf16[2,64,1024]{2,1,0:T(8,128)(2,1)S(1)}, bf16[2,64,1024]{2,1,0:T(8,128)(2,1)S(1)}, u32[]{:S(2)}, u32[]{:S(2)}) collective-permute-start(bf16[2,64,1024]{2,1,0:T(8,128)(2,1)S(1)} %get-tuple-element.752), channel_id=1, source_target_pairs={{1,0},{2,1},{3,2},{4,3},{5,4},{6,5},{7,6},{9,8},{10,9},{11,10},{12... | collective-permute-start | bytes 786440 | tf_op jit(solution)/shard_map/while/body/eval_jaxpr/ppermute | solution.py:18
  785.5 1.9 collective-permute-start.4
  788.8 4.7 collective-permute-done.4
  796.1 201.8 %collective-permute-start.5 = (bf16[2,64,4096]{2,1,0:T(8,128)(2,1)}, bf16[2,64,4096]{2,1,0:T(8,128)(2,1)S(1)}, u32[]{:S(2)}, u32[]{:S(2)}) collective-permute-start(bf16[2,64,4096]{2,1,0:T(8,128)(2,1)} %convert_element_type.125), channel_id=1, source_target_pairs={{0,8},{8,16},{16,24},{1,9},{9,17},{17,25},{2,10},{10,18},{18,26},{... | collective-permute-start | bytes 3145736 | tf_op jit(solution)/shard_map/while/body/eval_jaxpr/ppermute | solution.py:26
  998.0 12.0 collective-permute-done.5
  1010.0 3.1 select_dynamic-update-slice_fusion.4
  1013.2 41.8 %collective-permute-start.3 = (bf16[2,64,1024]{2,1,0:T(8,128)(2,1)S(1)}, bf16[2,64,1024]{2,1,0:T(8,128)(2,1)S(1)}, u32[]{:S(2)}, u32[]{:S(2)}) collective-permute-start(bf16[2,64,1024]{2,1,0:T(8,128)(2,1)S(1)} %get-tuple-element.752), channel_id=1, source_target_pairs={{1,0},{2,1},{3,2},{4,3},{5,4},{6,5},{7,6},{9,8},{10,9},{11,10},{12... | collective-permute-start | bytes 786440 | tf_op jit(solution)/shard_map/while/body/eval_jaxpr/ppermute | solution.py:18
  1055.0 1.9 collective-permute-start.4
  1058.3 4.7 collective-permute-done.4
  1065.6 5.7 collective-permute-start.5
  1071.3 12.0 collective-permute-done.5
  1085.0 1444.4 %while.88 = (s32[]{:T(128)}, bf16[2,64,4096]{2,1,0:T(8,128)(2,1)S(1)}, bf16[2,128,4096]{2,1,0:T(8,128)(2,1)}, s32[]{:T(128)}, s32[]{:T(128)}, /*index=5*/bf16[2,...) while((s32[]{:T(128)}, ...), condition=%wide.region_7.8_spmd, body=%wide.region_4.7_spmd.sunk | while | flops 140443664 | bytes 28312392 | solution.py:130
  1085.7 3.5 select_dynamic-update-slice_fusion.5
  1089.7 3.2 collective-permute-start
  1093.0 2.1 collective-permute-start.1
  1096.8 22.5 collective-permute-done.1
  1122.4 226.9 %collective-permute-done.2 = bf16[2,64,4096]{2,1,0:T(8,128)(2,1)S(1)} collective-permute-done((bf16[2,64,4096]{2,1,0:T(8,128)(2,1)}, bf16[2,64,4096]{2,1,0:T(8,128)(2,1)S(1)}, u32[]{:S(2)}, u32[]{:S(2)}) %collective-permute-start.2) | collective-permute-done | bytes 1048608 | tf_op jit(solution)/shard_map/while/body/eval_jaxpr/ppermute | solution.py:26
  1350.0 3.5 select_dynamic-update-slice_fusion.5
  1354.0 3.6 collective-permute-start
  1357.7 1.9 collective-permute-start.1
  1361.1 4.5 collective-permute-done.1
  1366.8 1.9 collective-permute-start.2
  1368.8 450.1 %collective-permute-done.2 = bf16[2,64,4096]{2,1,0:T(8,128)(2,1)S(1)} collective-permute-done((bf16[2,64,4096]{2,1,0:T(8,128)(2,1)}, bf16[2,64,4096]{2,1,0:T(8,128)(2,1)S(1)}, u32[]{:S(2)}, u32[]{:S(2)}) %collective-permute-start.2) | collective-permute-done | bytes 1048608 | tf_op jit(solution)/shard_map/while/body/eval_jaxpr/ppermute | solution.py:26
  1819.5 3.5 select_dynamic-update-slice_fusion.5
  1823.3 149.2 %while.90 = (s32[]{:T(128)}, f32[2,64,6144]{2,1,0:T(8,128)S(1)}, s32[]{:T(128)}, s32[24]{0:T(128)S(1)}, s32[24]{0:T(128)S(1)}, /*index=5*/bf16[2,64,4096]{2,1,0:...) while((s32[]{:T(128)}, f32[2,64,6144]{2,1,0:T(8,128)S(1)}, ...), condition=%wide.region_6.6_spmd, body=%wide.region_5.5_spmd.sunk | while | flops 134414336 | bytes 4194599 | solution.py:110
  1972.7 1.9 collective-permute-start
  1974.7 27.8 %collective-permute-start.1 = (bf16[2,64,1024]{2,1,0:T(8,128)(2,1)S(1)}, bf16[2,64,1024]{2,1,0:T(8,128)(2,1)S(1)}, u32[]{:S(2)}, u32[]{:S(2)}) collective-permute-start(bf16[2,64,1024]{2,1,0:T(8,128)(2,1)S(1)} %get-tuple-element.769), channel_id=1, source_target_pairs={{0,1},{1,2},{2,3},{3,4},{4,5},{5,6},{6,7},{8,9},{9,10},{10,11},{11... | collective-permute-start | bytes 786440 | tf_op jit(solution)/shard_map/while/body/eval_jaxpr/ppermute | solution.py:26
  2004.3 36.4 %collective-permute-done.1 = bf16[2,64,1024]{2,1,0:T(8,128)(2,1)S(1)} collective-permute-done((bf16[2,64,1024]{2,1,0:T(8,128)(2,1)S(1)}, bf16[2,64,1024]{2,1,0:T(8,128)(2,1)S(1)}, u32[]{:S(2)}, u32[]{:S(2)}) %collective-permute-start.1) | collective-permute-done | bytes 262176 | tf_op jit(solution)/shard_map/while/body/eval_jaxpr/ppermute | solution.py:26
  2043.8 33.8 %collective-permute-done.2 = bf16[2,64,4096]{2,1,0:T(8,128)(2,1)S(1)} collective-permute-done((bf16[2,64,4096]{2,1,0:T(8,128)(2,1)}, bf16[2,64,4096]{2,1,0:T(8,128)(2,1)S(1)}, u32[]{:S(2)}, u32[]{:S(2)}) %collective-permute-start.2) | collective-permute-done | bytes 1048608 | tf_op jit(solution)/shard_map/while/body/eval_jaxpr/ppermute | solution.py:26
  2078.2 3.5 select_dynamic-update-slice_fusion.5
  2082.0 149.2 %while.90 = (s32[]{:T(128)}, f32[2,64,6144]{2,1,0:T(8,128)S(1)}, s32[]{:T(128)}, s32[24]{0:T(128)S(1)}, s32[24]{0:T(128)S(1)}, /*index=5*/bf16[2,64,4096]{2,1,0:...) while((s32[]{:T(128)}, f32[2,64,6144]{2,1,0:T(8,128)S(1)}, ...), condition=%wide.region_6.6_spmd, body=%wide.region_5.5_spmd.sunk | while | flops 134414336 | bytes 4194599 | solution.py:110
  2231.5 1.9 collective-permute-start
  2233.4 28.1 %collective-permute-start.1 = (bf16[2,64,1024]{2,1,0:T(8,128)(2,1)S(1)}, bf16[2,64,1024]{2,1,0:T(8,128)(2,1)S(1)}, u32[]{:S(2)}, u32[]{:S(2)}) collective-permute-start(bf16[2,64,1024]{2,1,0:T(8,128)(2,1)S(1)} %get-tuple-element.769), channel_id=1, source_target_pairs={{0,1},{1,2},{2,3},{3,4},{4,5},{5,6},{6,7},{8,9},{9,10},{10,11},{11... | collective-permute-start | bytes 786440 | tf_op jit(solution)/shard_map/while/body/eval_jaxpr/ppermute | solution.py:26
  2261.5 7.0 collective-permute-done
  2268.5 28.4 %collective-permute-done.1 = bf16[2,64,1024]{2,1,0:T(8,128)(2,1)S(1)} collective-permute-done((bf16[2,64,1024]{2,1,0:T(8,128)(2,1)S(1)}, bf16[2,64,1024]{2,1,0:T(8,128)(2,1)S(1)}, u32[]{:S(2)}, u32[]{:S(2)}) %collective-permute-start.1) | collective-permute-done | bytes 262176 | tf_op jit(solution)/shard_map/while/body/eval_jaxpr/ppermute | solution.py:26
  2298.1 1.9 collective-permute-start.2
  2300.0 14.4 collective-permute-done.2
  2315.1 3.5 select_dynamic-update-slice_fusion.5
  2319.1 3.6 collective-permute-start
  2322.7 1.9 collective-permute-start.1
  2326.2 4.5 collective-permute-done.1
  2331.9 195.0 %collective-permute-start.2 = (bf16[2,64,4096]{2,1,0:T(8,128)(2,1)}, bf16[2,64,4096]{2,1,0:T(8,128)(2,1)S(1)}, u32[]{:S(2)}, u32[]{:S(2)}) collective-permute-start(bf16[2,64,4096]{2,1,0:T(8,128)(2,1)} %add_convert_fusion.6), channel_id=1, source_target_pairs={{8,0},{16,8},{24,16},{9,1},{17,9},{25,17},{10,2},{18,10},{26,18},{... | collective-permute-start | bytes 3145736 | tf_op jit(solution)/shard_map/while/body/eval_jaxpr/ppermute | solution.py:26
  2526.9 2.5 collective-permute-done.2
  (575 shorter events, 393.4 us)
Async XLA Ops:
  6.1 14.7 collective-permute-start.3
  9.2 11.7 collective-permute-start.4
  23.4 220.9 %collective-permute-start.5 = (bf16[2,64,4096]{2,1,0:T(8,128)(2,1)}, bf16[2,64,4096]{2,1,0:T(8,128)(2,1)S(1)}, u32[]{:S(2)}, u32[]{:S(2)}) collective-permute-start(bf16[2,64,4096]{2,1,0:T(8,128)(2,1)} %convert_element_type.125), channel_id=1, source_target_pairs={{0,8},{8,16},{16,24},{1,9},{9,17},{17,25},{2,10},{10,18},{18,26},{... | collective-permute-start | bytes 3145736 | tf_op jit(solution)/shard_map/while/body/eval_jaxpr/ppermute | solution.py:26
  247.5 15.3 collective-permute-start.3
  249.4 13.4 collective-permute-start.4
  422.2 63.4 %collective-permute-start.5 = (bf16[2,64,4096]{2,1,0:T(8,128)(2,1)}, bf16[2,64,4096]{2,1,0:T(8,128)(2,1)S(1)}, u32[]{:S(2)}, u32[]{:S(2)}) collective-permute-start(bf16[2,64,4096]{2,1,0:T(8,128)(2,1)} %convert_element_type.125), channel_id=1, source_target_pairs={{0,8},{8,16},{16,24},{1,9},{9,17},{17,25},{2,10},{10,18},{18,26},{... | collective-permute-start | bytes 3145736 | tf_op jit(solution)/shard_map/while/body/eval_jaxpr/ppermute | solution.py:26
  488.8 15.3 collective-permute-start.3
  490.8 13.4 collective-permute-start.4
  663.6 27.1 %collective-permute-start.5 = (bf16[2,64,4096]{2,1,0:T(8,128)(2,1)}, bf16[2,64,4096]{2,1,0:T(8,128)(2,1)S(1)}, u32[]{:S(2)}, u32[]{:S(2)}) collective-permute-start(bf16[2,64,4096]{2,1,0:T(8,128)(2,1)} %convert_element_type.125), channel_id=1, source_target_pairs={{0,8},{8,16},{16,24},{1,9},{9,17},{17,25},{2,10},{10,18},{18,26},{... | collective-permute-start | bytes 3145736 | tf_op jit(solution)/shard_map/while/body/eval_jaxpr/ppermute | solution.py:26
  693.8 95.0 %collective-permute-start.3 = (bf16[2,64,1024]{2,1,0:T(8,128)(2,1)S(1)}, bf16[2,64,1024]{2,1,0:T(8,128)(2,1)S(1)}, u32[]{:S(2)}, u32[]{:S(2)}) collective-permute-start(bf16[2,64,1024]{2,1,0:T(8,128)(2,1)S(1)} %get-tuple-element.752), channel_id=1, source_target_pairs={{1,0},{2,1},{3,2},{4,3},{5,4},{6,5},{7,6},{9,8},{10,9},{11,10},{12... | collective-permute-start | bytes 786440 | tf_op jit(solution)/shard_map/while/body/eval_jaxpr/ppermute | solution.py:18
  785.5 8.0 collective-permute-start.4
  796.1 213.9 %collective-permute-start.5 = (bf16[2,64,4096]{2,1,0:T(8,128)(2,1)}, bf16[2,64,4096]{2,1,0:T(8,128)(2,1)S(1)}, u32[]{:S(2)}, u32[]{:S(2)}) collective-permute-start(bf16[2,64,4096]{2,1,0:T(8,128)(2,1)} %convert_element_type.125), channel_id=1, source_target_pairs={{0,8},{8,16},{16,24},{1,9},{9,17},{17,25},{2,10},{10,18},{18,26},{... | collective-permute-start | bytes 3145736 | tf_op jit(solution)/shard_map/while/body/eval_jaxpr/ppermute | solution.py:26
  1013.2 45.1 %collective-permute-start.3 = (bf16[2,64,1024]{2,1,0:T(8,128)(2,1)S(1)}, bf16[2,64,1024]{2,1,0:T(8,128)(2,1)S(1)}, u32[]{:S(2)}, u32[]{:S(2)}) collective-permute-start(bf16[2,64,1024]{2,1,0:T(8,128)(2,1)S(1)} %get-tuple-element.752), channel_id=1, source_target_pairs={{1,0},{2,1},{3,2},{4,3},{5,4},{6,5},{7,6},{9,8},{10,9},{11,10},{12... | collective-permute-start | bytes 786440 | tf_op jit(solution)/shard_map/while/body/eval_jaxpr/ppermute | solution.py:18
  1055.0 8.0 collective-permute-start.4
  1065.6 17.7 collective-permute-start.5
  1089.7 7.1 collective-permute-start
  1093.0 26.3 %collective-permute-start.1 = (bf16[2,64,1024]{2,1,0:T(8,128)(2,1)S(1)}, bf16[2,64,1024]{2,1,0:T(8,128)(2,1)S(1)}, u32[]{:S(2)}, u32[]{:S(2)}) collective-permute-start(bf16[2,64,1024]{2,1,0:T(8,128)(2,1)S(1)} %get-tuple-element.769), channel_id=1, source_target_pairs={{0,1},{1,2},{2,3},{3,4},{4,5},{5,6},{6,7},{8,9},{9,10},{10,11},{11... | collective-permute-start | bytes 786440 | tf_op jit(solution)/shard_map/while/body/eval_jaxpr/ppermute | solution.py:26
  1120.5 228.8 %collective-permute-start.2 = (bf16[2,64,4096]{2,1,0:T(8,128)(2,1)}, bf16[2,64,4096]{2,1,0:T(8,128)(2,1)S(1)}, u32[]{:S(2)}, u32[]{:S(2)}) collective-permute-start(bf16[2,64,4096]{2,1,0:T(8,128)(2,1)} %add_convert_fusion.6), channel_id=1, source_target_pairs={{8,0},{16,8},{24,16},{9,1},{17,9},{25,17},{10,2},{18,10},{26,18},{... | collective-permute-start | bytes 3145736 | tf_op jit(solution)/shard_map/while/body/eval_jaxpr/ppermute | solution.py:26
  1354.0 7.1 collective-permute-start
  1357.7 8.0 collective-permute-start.1
  1366.8 452.0 %collective-permute-start.2 = (bf16[2,64,4096]{2,1,0:T(8,128)(2,1)}, bf16[2,64,4096]{2,1,0:T(8,128)(2,1)S(1)}, u32[]{:S(2)}, u32[]{:S(2)}) collective-permute-start(bf16[2,64,4096]{2,1,0:T(8,128)(2,1)} %add_convert_fusion.6), channel_id=1, source_target_pairs={{8,0},{16,8},{24,16},{9,1},{17,9},{25,17},{10,2},{18,10},{26,18},{... | collective-permute-start | bytes 3145736 | tf_op jit(solution)/shard_map/while/body/eval_jaxpr/ppermute | solution.py:26
  1972.7 31.5 %collective-permute-start = (bf16[2,64,1024]{2,1,0:T(8,128)(2,1)S(1)}, bf16[2,64,1024]{2,1,0:T(8,128)(2,1)S(1)}, u32[]{:S(2)}, u32[]{:S(2)}) collective-permute-start(bf16[2,64,1024]{2,1,0:T(8,128)(2,1)S(1)} %get-tuple-element.768), channel_id=1, source_target_pairs={{1,0},{2,1},{3,2},{4,3},{5,4},{6,5},{7,6},{9,8},{10,9},{11,10},{12... | collective-permute-start | bytes 786440 | tf_op jit(solution)/shard_map/while/body/eval_jaxpr/ppermute | solution.py:26
  1974.7 66.0 %collective-permute-start.1 = (bf16[2,64,1024]{2,1,0:T(8,128)(2,1)S(1)}, bf16[2,64,1024]{2,1,0:T(8,128)(2,1)S(1)}, u32[]{:S(2)}, u32[]{:S(2)}) collective-permute-start(bf16[2,64,1024]{2,1,0:T(8,128)(2,1)S(1)} %get-tuple-element.769), channel_id=1, source_target_pairs={{0,1},{1,2},{2,3},{3,4},{4,5},{5,6},{6,7},{8,9},{9,10},{10,11},{11... | collective-permute-start | bytes 786440 | tf_op jit(solution)/shard_map/while/body/eval_jaxpr/ppermute | solution.py:26
  2041.9 35.7 %collective-permute-start.2 = (bf16[2,64,4096]{2,1,0:T(8,128)(2,1)}, bf16[2,64,4096]{2,1,0:T(8,128)(2,1)S(1)}, u32[]{:S(2)}, u32[]{:S(2)}) collective-permute-start(bf16[2,64,4096]{2,1,0:T(8,128)(2,1)} %add_convert_fusion.6), channel_id=1, source_target_pairs={{8,0},{16,8},{24,16},{9,1},{17,9},{25,17},{10,2},{18,10},{26,18},{... | collective-permute-start | bytes 3145736 | tf_op jit(solution)/shard_map/while/body/eval_jaxpr/ppermute | solution.py:26
  2231.5 37.1 %collective-permute-start = (bf16[2,64,1024]{2,1,0:T(8,128)(2,1)S(1)}, bf16[2,64,1024]{2,1,0:T(8,128)(2,1)S(1)}, u32[]{:S(2)}, u32[]{:S(2)}) collective-permute-start(bf16[2,64,1024]{2,1,0:T(8,128)(2,1)S(1)} %get-tuple-element.768), channel_id=1, source_target_pairs={{1,0},{2,1},{3,2},{4,3},{5,4},{6,5},{7,6},{9,8},{10,9},{11,10},{12... | collective-permute-start | bytes 786440 | tf_op jit(solution)/shard_map/while/body/eval_jaxpr/ppermute | solution.py:26
  2233.4 63.5 %collective-permute-start.1 = (bf16[2,64,1024]{2,1,0:T(8,128)(2,1)S(1)}, bf16[2,64,1024]{2,1,0:T(8,128)(2,1)S(1)}, u32[]{:S(2)}, u32[]{:S(2)}) collective-permute-start(bf16[2,64,1024]{2,1,0:T(8,128)(2,1)S(1)} %get-tuple-element.769), channel_id=1, source_target_pairs={{0,1},{1,2},{2,3},{3,4},{4,5},{5,6},{6,7},{8,9},{9,10},{10,11},{11... | collective-permute-start | bytes 786440 | tf_op jit(solution)/shard_map/while/body/eval_jaxpr/ppermute | solution.py:26
  2298.1 16.3 collective-permute-start.2
  2319.1 7.1 collective-permute-start
  2322.7 8.0 collective-permute-start.1
  2331.9 197.5 %collective-permute-start.2 = (bf16[2,64,4096]{2,1,0:T(8,128)(2,1)}, bf16[2,64,4096]{2,1,0:T(8,128)(2,1)S(1)}, u32[]{:S(2)}, u32[]{:S(2)}) collective-permute-start(bf16[2,64,4096]{2,1,0:T(8,128)(2,1)} %add_convert_fusion.6), channel_id=1, source_target_pairs={{8,0},{16,8},{24,16},{9,1},{17,9},{25,17},{10,2},{18,10},{26,18},{... | collective-permute-start | bytes 3145736 | tf_op jit(solution)/shard_map/while/body/eval_jaxpr/ppermute | solution.py:26
where the time goes:
time: 2550 us; the launch traced here: 2530 us
  waiting for transfers between devices  1190 us (47%)
  starting transfers between devices  661 us (26%)
  loops' own time  265 us (10%)
  local copies, waits for them, and re-layouts  181 us (7%)
  matrix products  168 us (7%)
  other arithmetic  64 us (3%)
    ppermute x20, waiting for transfers between devices, from_behind(): return lax.ppermute(block, axis, route)  1150 us
    ppermute x20, starting transfers between devices, from_behind(): return lax.ppermute(block, axis, route)  508 us
    ppermute x5, starting transfers between devices, padded(): after = lax.ppermute(initial, axis, down)  140 us
    another operation x5, loops' own time, down_step(): lax.fori_loop(0, jnp.where(active, live_count, 0), down_add_tile, jnp.zer...  134 us
    another operation x5, loops' own time, up_step(): lax.fori_loop(0, jnp.where(active, live_count, 0), up_add_tile, jnp.zeros...  124 us
    dot_general x64, matrix products, complex_apply(): lax.dot_general(flattened, matrix[1], numbers, preferred_element_type=jnp...  83.9 us
    dot_general x64, matrix products, complex_apply(): lax.dot_general(flattened, matrix[0], numbers, preferred_element_type=jnp...  83.9 us
  transfers between devices with their start and end apart: 30, of which 27 were waited for; matrix products, arithmetic and copies ran while one was open for 0% of the time, Pallas kernels for 0%

commit v1 on v0

v1 whole, which is shorter than its diff:
```python
import functools

import jax
import jax.numpy as jnp
from jax import lax
from jax.experimental import pallas as pl
from jax.experimental.pallas import tpu as pltpu
from jax.sharding import PartitionSpec as P

BAND = 2
MESH = pl.DeviceIdType.MESH


def block_order(n):
    if n <= 2 * BAND:
        return list(range(n))
    return list(range(BAND)) + list(range(n - BAND, n)) + list(range(BAND, n - BAND))


def sorted_by(key, values):
    rank = jnp.sum(key[None, :] < key[:, None], axis=1)
    slots = key.shape[0]
    place = rank[None, :] == jnp.arange(slots)[:, None]
    return [jnp.sum(jnp.where(place, v[None, :], 0), axis=1) for v in values]


def chain(group, alive, first, base, groups):
    slots = group.shape[0]
    at = jnp.arange(slots, dtype=jnp.int32)
    same = jnp.concatenate([jnp.zeros((1,), bool), (group[1:] == group[:-1]) & (alive[1:] > 0)])
    prev = jnp.where(same, base + at - 1, first(group))
    member = (group[None, :] == jnp.arange(groups)[:, None]) & (alive[None, :] > 0)
    last = jnp.max(jnp.where(member, base + at[None, :], -1), axis=1)
    return prev, last


def plan(rows, cols, count, first_block, n):
    slots = rows.shape[0]
    ids = jnp.arange(slots, dtype=jnp.int32)
    r = rows - first_block
    c = cols - first_block + BAND
    live = ids < count
    diag = live & (c == r + BAND)
    dslot = jnp.sum(
        jnp.where(diag[None, :] & (r[None, :] == jnp.arange(n)[:, None]), ids[None, :], 0), axis=1
    )
    order = block_order(n)
    prio_r = [0] * n
    for p, b in enumerate(order):
        prio_r[b] = p
    rank_r = sum(jnp.where(r == b, prio_r[b], 0) for b in range(n))
    big = 64 * slots
    key = jnp.where(diag, 2 * big, jnp.where(live, rank_r * slots, big)) + ids
    s_ids, s_r, s_c, s_live = sorted_by(key, [ids, r, c, live.astype(jnp.int32)])
    rest = slots - n
    d_ord, d_r, d_c, d_live = s_ids[:rest], s_r[:rest], s_c[:rest], s_live[:rest]
    d_prev, d_last = chain(d_r, d_live, lambda g: g, n, n)
    d_last = jnp.where(d_last < 0, jnp.arange(n), d_last)
    wide = n + 2 * BAND
    order_c = list(range(BAND)) + list(range(wide - BAND, wide))
    order_c += [b for b in range(2 * BAND, n)] + [
        b for b in range(BAND, n + BAND) if not 2 * BAND <= b < n
    ]
    prio_c = [0] * wide
    for p, b in enumerate(order_c):
        prio_c[b] = p
    rank_c = sum(jnp.where(c == b, prio_c[b], 0) for b in range(wide))
    key = jnp.where(live, rank_c * slots, big) + ids
    u_ord, u_row, u_col, u_live = sorted_by(key, [ids, r, c, live.astype(jnp.int32)])
    u_prev, u_last = chain(u_col, u_live, lambda g: jnp.full_like(g, slots), 0, wide)
    u_last = jnp.where(u_last < 0, slots, u_last)
    parts = [dslot, d_ord, d_c, d_prev, d_last, u_ord, u_row, u_prev, u_last]
    offsets, at = [], 0
    for p in parts:
        offsets.append(at)
        at += p.shape[0]
    return jnp.concatenate([p.astype(jnp.int32) for p in parts]), offsets


def kernel(
    layers, groups, n, slots, offsets,
    idx, source, tiles_hbm, down_out, up_out,
    tiles, acc, src, ext, up, inc, binc, snd, bsnd, rim_snd, rim_rcv,
    tile_sem, src_sem, out_sem, inc_send, inc_recv, binc_send, binc_recv,
    halo_send, halo_recv, rim_send, rim_recv,
):
    o_dslot, o_dord, o_dcol, o_dprev, o_dlast, o_uord, o_urow, o_uprev, o_ulast = offsets
    half, tile = src.shape[2], src.shape[3]
    layer = lax.axis_index("layer")
    blk = lax.axis_index("blk")
    has_prev, has_next = layer > 0, layer < layers - 1
    has_left, has_right = blk > 0, blk < groups - 1
    to_prev, to_next = (layer - 1, blk), (layer + 1, blk)
    to_left, to_right = (layer, blk - 1), (layer, blk + 1)
    partners = ((has_prev, to_prev), (has_next, to_next), (has_left, to_left), (has_right, to_right))

    def tile_copy(s):
        return pltpu.make_async_copy(tiles_hbm.at[s], tiles.at[s], tile_sem.at[s])

    def src_copy(b):
        return pltpu.make_async_copy(
            source.at[:, :, pl.ds(b * tile, tile)], src.at[b], src_sem.at[b]
        )

    def down_copy(b):
        return pltpu.make_async_copy(
            ext.at[BAND + b], down_out.at[:, :, pl.ds(b * tile, tile)], out_sem.at[0, b]
        )

    def up_copy(b):
        return pltpu.make_async_copy(
            up.at[b], up_out.at[:, :, pl.ds(b * tile, tile)], out_sem.at[1, b]
        )

    def fwd_copy(b):
        return pltpu.make_async_remote_copy(
            src_ref=snd.at[b], dst_ref=inc.at[b], send_sem=inc_send.at[b],
            recv_sem=inc_recv.at[b], device_id=to_next, device_id_type=MESH,
        )

    def bwd_copy(b):
        return pltpu.make_async_remote_copy(
            src_ref=bsnd.at[b], dst_ref=binc.at[b], send_sem=binc_send.at[b],
            recv_sem=binc_recv.at[b], device_id=to_prev, device_id_type=MESH,
        )

    def halo_copy(side):
        if side == 0:
            a, b, dev = ext.at[pl.ds(BAND, BAND)], ext.at[pl.ds(BAND + n, BAND)], to_left
        else:
            a, b, dev = ext.at[pl.ds(n, BAND)], ext.at[pl.ds(0, BAND)], to_right
        return pltpu.make_async_remote_copy(
            src_ref=a, dst_ref=b, send_sem=halo_send.at[side],
            recv_sem=halo_recv.at[side], device_id=dev, device_id_type=MESH,
        )

    def rim_copy(side):
        return pltpu.make_async_remote_copy(
            src_ref=rim_snd.at[side], dst_ref=rim_rcv.at[side], send_sem=rim_send.at[side],
            recv_sem=rim_recv.at[side], device_id=(to_left, to_right)[side], device_id_type=MESH,
        )

    for b in block_order(n):
        src_copy(b).start()

    @pl.loop(0, slots)
    def _(s):
        tile_copy(s).start()

    barrier = pltpu.get_barrier_semaphore()
    for there, dev in partners:
        @pl.when(there)
        def _(dev=dev):
            pl.semaphore_signal(barrier, inc=1, device_id=dev, device_id_type=MESH)
    pl.semaphore_wait(barrier, sum(there.astype(jnp.int32) for there, _ in partners))

    def product(x, s, dim, write):
        x1 = x.reshape(2 * half, tile)
        x2 = jnp.concatenate([-x[1], x[0]], axis=0)
        numbers = (((1,), (dim,)), ((), ()))
        step = min(tile, 256)
        for j in range(0, tile, step):
            if dim == 1:
                real, imag = tiles[s, 0, j:j + step, :], tiles[s, 1, j:j + step, :]
            else:
                real, imag = tiles[s, 0, :, j:j + step], tiles[s, 1, :, j:j + step]
            y = lax.dot_general(x1, real, numbers, preferred_element_type=jnp.float32)
            y = y + lax.dot_general(x2, imag, numbers, preferred_element_type=jnp.float32)
            write(slice(j, j + step), y)

    @pl.when(jnp.logical_not(has_left))
    def _():
        ext[0:BAND] = jnp.zeros((BAND,) + ext.shape[1:], ext.dtype)
        rim_rcv[1] = jnp.zeros(rim_rcv.shape[1:], rim_rcv.dtype)

    @pl.when(jnp.logical_not(has_right))
    def _():
        ext[BAND + n:] = jnp.zeros((BAND,) + ext.shape[1:], ext.dtype)
        rim_rcv[0] = jnp.zeros(rim_rcv.shape[1:], rim_rcv.dtype)

    for p, b in enumerate(block_order(n)):
        src_copy(b).wait()

        @pl.when(has_prev)
        def _(b=b):
            fwd_copy(b).wait_recv()
            total = src[b].astype(jnp.float32) + inc[b].astype(jnp.float32)
            ext[BAND + b] = total.astype(jnp.bfloat16)

        @pl.when(jnp.logical_not(has_prev))
        def _(b=b):
            ext[BAND + b] = src[b]

        if p == min(n, 2 * BAND) - 1:
            for side, there in enumerate((has_left, has_right)):
                @pl.when(has_next & there)
                def _(side=side):
                    halo_copy(side).start()
        down_copy(b).start()

    @pl.loop(0, slots)
    def _(s):
        tile_copy(s).wait()

    @pl.when(has_next)
    def _():
        @pl.loop(0, n)
        def _(r):
            def write(at, y):
                acc[r, :, at] = y

            product(ext[BAND + r], idx[o_dslot + r], 1, write)

        for side, there in enumerate((has_right, has_left)):
            @pl.when(there)
            def _(side=side):
                halo_copy(side).wait_recv()

        @pl.loop(0, slots - n)
        def _(k):
            before = idx[o_dprev + k]

            def write(at, y):
                acc[n + k, :, at] = acc[before, :, at] + y

            product(ext[idx[o_dcol + k]], idx[o_dord + k], 1, write)

        for b in block_order(n):
            snd[b] = acc[idx[o_dlast + b]].astype(jnp.bfloat16).reshape(snd.shape[1:])
            fwd_copy(b).start()

    for b in range(n):
        @pl.when(has_next)
        def _(b=b):
            bwd_copy(b).wait_recv()
            total = ext[BAND + b].astype(jnp.float32) + binc[b].astype(jnp.float32)
            up[b] = total.astype(jnp.bfloat16)

        @pl.when(jnp.logical_not(has_next))
        def _(b=b):
            up[b] = ext[BAND + b]

        up_copy(b).start()

    @pl.when(has_prev)
    def _():
        acc[slots] = jnp.zeros(acc.shape[1:], acc.dtype)

        def slot(k):
            before = idx[o_uprev + k]

            def write(at, y):
                acc[k, :, at] = acc[before, :, at] + y

            product(up[idx[o_urow + k]], idx[o_uord + k], 0, write)

        rims = min(slots, BAND * (BAND + 1))
        pl.loop(0, rims)(slot)
        for side, there in enumerate((has_left, has_right)):
            for b in range(BAND):
                c = b if side == 0 else BAND + n + b
                rim_snd[side, b] = (
                    acc[idx[o_ulast + c]].astype(jnp.bfloat16).reshape(rim_snd.shape[2:])
                )

            @pl.when(there)
            def _(side=side):
                rim_copy(side).start()
        pl.loop(rims, slots)(slot)
        inside = [b for b in range(n) if BAND <= b < n - BAND]
        border = [b for b in range(n) if b not in inside]
        for b in inside:
            bsnd[b] = acc[idx[o_ulast + BAND + b]].astype(jnp.bfloat16).reshape(bsnd.shape[1:])
            bwd_copy(b).start()
        for side, there in enumerate((has_right, has_left)):
            @pl.when(there)
            def _(side=side):
                rim_copy(side).wait_recv()
        for b in border:
            total = acc[idx[o_ulast + BAND + b]].reshape(bsnd.shape[1:])
            if b < BAND:
                total = total + rim_rcv[1, b].astype(jnp.float32)
            if b >= n - BAND:
                total = total + rim_rcv[0, b - (n - BAND)].astype(jnp.float32)
            bsnd[b] = total.astype(jnp.bfloat16)
            bwd_copy(b).start()

    for b in range(n):
        down_copy(b).wait()
        up_copy(b).wait()

        @pl.when(has_next)
        def _(b=b):
            fwd_copy(b).wait_send()

        @pl.when(has_prev)
        def _(b=b):
            bwd_copy(b).wait_send()
    for side, there in enumerate((has_left, has_right)):
        @pl.when(has_next & there)
        def _(side=side):
            halo_copy(side).wait_send()

        @pl.when(has_prev & there)
        def _(side=side):
            rim_copy(side).wait_send()


def on_device(source, tile_data, tile_rows, tile_cols, tile_count):
    layers, groups = lax.axis_size("layer"), lax.axis_size("blk")
    slots, tile = tile_data.shape[1], tile_data.shape[3]
    _, parts, half, length = source.shape
    n = length // tile
    idx, offsets = plan(tile_rows[0], tile_cols[0], tile_count[0, 0], lax.axis_index("blk") * n, n)
    block = (parts, half, tile)
    bf16 = jnp.bfloat16
    dma = pltpu.SemaphoreType.DMA
    shape = jax.ShapeDtypeStruct((parts, half, length), bf16)
    down, up = pl.pallas_call(
        functools.partial(kernel, layers, groups, n, slots, offsets),
        out_shape=(shape, shape),
        in_specs=[
            pl.BlockSpec(memory_space=pltpu.SMEM),
            pl.BlockSpec(memory_space=pl.ANY),
            pl.BlockSpec(memory_space=pl.ANY),
        ],
        out_specs=(pl.BlockSpec(memory_space=pl.ANY), pl.BlockSpec(memory_space=pl.ANY)),
        scratch_shapes=[
            pltpu.VMEM((slots, 2, tile, tile), bf16),
            pltpu.VMEM((slots + 1, parts * half, tile), jnp.float32),
            pltpu.VMEM((n,) + block, bf16),
            pltpu.VMEM((n + 2 * BAND,) + block, bf16),
            pltpu.VMEM((n,) + block, bf16),
            pltpu.VMEM((n,) + block, bf16),
            pltpu.VMEM((n,) + block, bf16),
            pltpu.VMEM((n,) + block, bf16),
            pltpu.VMEM((n,) + block, bf16),
            pltpu.VMEM((2, BAND) + block, bf16),
            pltpu.VMEM((2, BAND) + block, bf16),
            dma((slots,)),
            dma((n,)),
            dma((2, n)),
            dma((n,)),
            dma((n,)),
            dma((n,)),
            dma((n,)),
            dma((2,)),
            dma((2,)),
            dma((2,)),
            dma((2,)),
        ],
        compiler_params=pltpu.CompilerParams(
            collective_id=0, has_side_effects=True, vmem_limit_bytes=62 * 1024 * 1024
        ),
    )(idx, source[0], tile_data[0])
    return (down[None], up[None])


def solution(mesh):
    in_specs = (
        P("layer", None, None, "blk"),
        P("layer", "blk", None, None, None),
        P("layer", "blk"),
        P("layer", "blk"),
        P("layer", "blk"),
    )
    out_specs = (P("layer", None, None, "blk"), P("layer", None, None, "blk"))
    return jax.shard_map(
        on_device, mesh=mesh, in_specs=in_specs, out_specs=out_specs, check_vma=False
    )
```

time: 2550 us -> 172 us (0.07)
  the two profiles are of different devices: /device:TPU:25 before, /device:TPU:16 now
where the time goes in v1:
time: 172 us
  Pallas kernels  163 us (95%)
  local copies, waits for them, and re-layouts  5.25 us (3%)
  other arithmetic  2.67 us (2%)
    pallas_call x1, Pallas kernels, on_device(): pl.pallas_call(functools.partial(kernel, layers, groups, n, slots, offset...  163 us
    unnamed x4, local copies, waits for them, and re-layouts  4.6 us

profile of v1, /device:TPU:16, one launch (start us, length us, event | category | flops | bytes accessed | tf_op | source)
XLA Modules:
  0.0 172.0 jit_solution(14826111603518176987)
XLA Ops:
  1.3 0.7 fusion.27
  2.0 0.7 fusion.23
  2.7 0.2 convert_reduce_fusion
  2.9 0.2 convert_reduce_fusion.1
  3.1 0.1 select_reduce_fusion.10
  3.2 0.2 select_reduce_fusion.1
  3.4 0.1 compare_and_fusion
  3.5 0.1 select_reduce_fusion.8
  3.6 0.1 add_select_fusion.1
  3.7 0.1 compare_and_fusion.1
  3.8 0.1 fusion.31
  3.9 0.1 select_reduce_fusion.9
  4.0 0.7 concatenate.11.idx
  4.7 162.8 %shard_map.68 = (bf16[2,128,4096]{2,1,0:T(8,128)(2,1)}, bf16[2,128,4096]{2,1,0:T(8,128)(2,1)}) custom-call(s32[148]{0:T(256)} %concatenate.11.idx, bf16[2,128,4096]{2,1,0:T(8,128)(2,1)} %bitcast.38, bf16[24,2,512,512]{3,2,1,0:T(8,128)(2,1)} %bitcast.35), custom_call_target="tpu_custom_call" | custom-call | tf_op jit(solution)/shard_map/pallas_call | solution.py:319
  167.4 0.0 copy-start
  167.4 3.3 %copy.10 = bf16[1,2,128,4096]{3,2,1,0:T(8,128)(2,1)} copy(bf16[1,2,128,4096]{3,2,1,0:T(8,128)(2,1)} %bitcast.37) | data formatting | bytes 4194304
  170.7 0.0 copy-done
  170.7 1.3 copy.11
  (8 shorter events, 0.0 us)
Async XLA Ops:
  167.4 3.3 %copy-start = (bf16[2,128,4096]{2,1,0:T(8,128)(2,1)S(1)}, bf16[2,128,4096]{2,1,0:T(8,128)(2,1)}, u32[]{:S(2)}) copy-start(bf16[2,128,4096]{2,1,0:T(8,128)(2,1)} %get-tuple-element.5) | copy-start | bytes 6291460

commit v2 on v1

--- a/solution.py
+++ b/solution.py
@@ -11,65 +11,51 @@
 MESH = pl.DeviceIdType.MESH
 
 
-def block_order(n):
-    if n <= 2 * BAND:
-        return list(range(n))
-    return list(range(BAND)) + list(range(n - BAND, n)) + list(range(BAND, n - BAND))
+SPAN = 2 * BAND + 1
+RIMS = BAND * (BAND + 1)
+CHUNK = 2 * BAND
+
+
+def down_block(p, n):
+    return (p + n - BAND) % n
+
+
+def up_block(p, n):
+    return (p + n // 2) % n
 
 
 def sorted_by(key, values):
-    rank = jnp.sum(key[None, :] < key[:, None], axis=1)
     slots = key.shape[0]
+    rank = jnp.sum(key[None, :] < key[:, None], axis=1).astype(jnp.int32)
     place = rank[None, :] == jnp.arange(slots)[:, None]
-    return [jnp.sum(jnp.where(place, v[None, :], 0), axis=1) for v in values]
-
-
-def chain(group, alive, first, base, groups):
-    slots = group.shape[0]
-    at = jnp.arange(slots, dtype=jnp.int32)
-    same = jnp.concatenate([jnp.zeros((1,), bool), (group[1:] == group[:-1]) & (alive[1:] > 0)])
-    prev = jnp.where(same, base + at - 1, first(group))
-    member = (group[None, :] == jnp.arange(groups)[:, None]) & (alive[None, :] > 0)
-    last = jnp.max(jnp.where(member, base + at[None, :], -1), axis=1)
-    return prev, last
-
-
-def plan(rows, cols, count, first_block, n):
+    return rank, jnp.sum(jnp.where(place[None], values[:, None, :], 0), axis=2)
+
+
+def plan(rows, cols, count, first_block, n, rest):
     slots = rows.shape[0]
     ids = jnp.arange(slots, dtype=jnp.int32)
     r = rows - first_block
-    c = cols - first_block + BAND
+    c = cols - first_block
     live = ids < count
-    diag = live & (c == r + BAND)
-    dslot = jnp.sum(
-        jnp.where(diag[None, :] & (r[None, :] == jnp.arange(n)[:, None]), ids[None, :], 0), axis=1
-    )
-    order = block_order(n)
-    prio_r = [0] * n
-    for p, b in enumerate(order):
-        prio_r[b] = p
-    rank_r = sum(jnp.where(r == b, prio_r[b], 0) for b in range(n))
-    big = 64 * slots
-    key = jnp.where(diag, 2 * big, jnp.where(live, rank_r * slots, big)) + ids
-    s_ids, s_r, s_c, s_live = sorted_by(key, [ids, r, c, live.astype(jnp.int32)])
-    rest = slots - n
-    d_ord, d_r, d_c, d_live = s_ids[:rest], s_r[:rest], s_c[:rest], s_live[:rest]
-    d_prev, d_last = chain(d_r, d_live, lambda g: g, n, n)
-    d_last = jnp.where(d_last < 0, jnp.arange(n), d_last)
-    wide = n + 2 * BAND
-    order_c = list(range(BAND)) + list(range(wide - BAND, wide))
-    order_c += [b for b in range(2 * BAND, n)] + [
-        b for b in range(BAND, n + BAND) if not 2 * BAND <= b < n
-    ]
-    prio_c = [0] * wide
-    for p, b in enumerate(order_c):
-        prio_c[b] = p
-    rank_c = sum(jnp.where(c == b, prio_c[b], 0) for b in range(wide))
-    key = jnp.where(live, rank_c * slots, big) + ids
-    u_ord, u_row, u_col, u_live = sorted_by(key, [ids, r, c, live.astype(jnp.int32)])
-    u_prev, u_last = chain(u_col, u_live, lambda g: jnp.full_like(g, slots), 0, wide)
-    u_last = jnp.where(u_last < 0, slots, u_last)
-    parts = [dslot, d_ord, d_c, d_prev, d_last, u_ord, u_row, u_prev, u_last]
+    diag = live & (c == r)
+    left, right = c < 0, c >= n
+    rim = live & (left | right)
+    big = n * slots
+    key = jnp.where(live, ((r + BAND) % n) * slots, big) + ids
+    key = jnp.where(diag, key + 2 * big, key)
+    rank, (d_ord, d_col) = sorted_by(key, jnp.stack([ids, c + BAND]))
+    d_pos = jnp.where(diag, r, n + rank)
+    key = jnp.where(live, ((c + n - n // 2) % n) * slots, big) + ids
+    key = jnp.where(diag | rim, key + 2 * big, key)
+    rank, (u_ord, u_row) = sorted_by(key, jnp.stack([ids, r]))
+    rim_at = jnp.where(left, r + c + BAND, RIMS // 2 + r + BAND - n + c - n)
+    u_pos = jnp.where(diag, r, n + jnp.where(rim, rim_at, RIMS + rank))
+    zero = max(slots, n + RIMS + rest)
+    place = r * SPAN + c - r + BAND
+    match = live[:, None] & (place[:, None] == jnp.arange(n * SPAN)[None, :])
+    values = jnp.stack([ids, d_pos - zero, u_pos - zero])
+    table, d_at, u_at = jnp.sum(jnp.where(match[None], values[:, :, None], 0), axis=1)
+    parts = [table, d_at + zero, u_at + zero, d_ord, d_col, u_ord, u_row]
     offsets, at = [], 0
     for p in parts:
         offsets.append(at)
@@ -78,13 +64,14 @@
 
 
 def kernel(
-    layers, groups, n, slots, offsets,
+    layers, groups, n, slots, rest, offsets,
     idx, source, tiles_hbm, down_out, up_out,
     tiles, acc, src, ext, up, inc, binc, snd, bsnd, rim_snd, rim_rcv,
     tile_sem, src_sem, out_sem, inc_send, inc_recv, binc_send, binc_recv,
     halo_send, halo_recv, rim_send, rim_recv,
 ):
-    o_dslot, o_dord, o_dcol, o_dprev, o_dlast, o_uord, o_urow, o_uprev, o_ulast = offsets
+    o_table, o_dat, o_uat, o_dord, o_dcol, o_uord, o_urow = offsets
+    zero = acc.shape[0] - 1
     half, tile = src.shape[2], src.shape[3]
     layer = lax.axis_index("layer")
     blk = lax.axis_index("blk")
@@ -140,8 +127,8 @@
             recv_sem=rim_recv.at[side], device_id=(to_left, to_right)[side], device_id_type=MESH,
         )
 
-    for b in block_order(n):
-        src_copy(b).start()
+    for p in range(n):
+        src_copy(down_block(p, n)).start()
 
     @pl.loop(0, slots)
     def _(s):
@@ -178,112 +165,178 @@
         ext[BAND + n:] = jnp.zeros((BAND,) + ext.shape[1:], ext.dtype)
         rim_rcv[0] = jnp.zeros(rim_rcv.shape[1:], rim_rcv.dtype)
 
-    for p, b in enumerate(block_order(n)):
+    acc[zero] = jnp.zeros(acc.shape[1:], acc.dtype)
+
+    def keep(place):
+        def write(at, y):
+            acc[place, :, at] = y
+
+        return write
+
+    def chunked(total, slot, after):
+        @pl.loop(0, total // CHUNK)
+        def _(p):
+            for j in range(CHUNK):
+                slot(p * CHUNK + j)
+            after(p)
+
+        for k in range(total // CHUNK * CHUNK, total):
+            slot(k)
+
+    @pl.loop(0, slots)
+    def _(s):
+        tile_copy(s).wait()
+
+    border = min(n, 2 * BAND)
+
+    def down_arrival(p):
+        b = down_block(p, n)
         src_copy(b).wait()
 
         @pl.when(has_prev)
-        def _(b=b):
+        def _():
             fwd_copy(b).wait_recv()
             total = src[b].astype(jnp.float32) + inc[b].astype(jnp.float32)
             ext[BAND + b] = total.astype(jnp.bfloat16)
 
         @pl.when(jnp.logical_not(has_prev))
-        def _(b=b):
+        def _():
             ext[BAND + b] = src[b]
 
-        if p == min(n, 2 * BAND) - 1:
-            for side, there in enumerate((has_left, has_right)):
-                @pl.when(has_next & there)
-                def _(side=side):
-                    halo_copy(side).start()
         down_copy(b).start()
 
-    @pl.loop(0, slots)
-    def _(s):
-        tile_copy(s).wait()
+    def down_diagonal(p):
+        b = down_block(p, n)
+        product(ext[BAND + b], idx[o_table + b * SPAN + BAND], 1, keep(b))
+
+    pl.loop(0, border)(down_arrival)
+    for side, there in enumerate((has_left, has_right)):
+        @pl.when(has_next & there)
+        def _(side=side):
+            halo_copy(side).start()
 
     @pl.when(has_next)
     def _():
-        @pl.loop(0, n)
-        def _(r):
-            def write(at, y):
-                acc[r, :, at] = y
-
-            product(ext[BAND + r], idx[o_dslot + r], 1, write)
-
+        pl.loop(0, border)(down_diagonal)
+
+    @pl.loop(border, n)
+    def _(p):
+        down_arrival(p)
+
+        @pl.when(has_next)
+        def _():
+            down_diagonal(p)
+
+    @pl.when(has_next)
+    def _():
         for side, there in enumerate((has_right, has_left)):
             @pl.when(there)
             def _(side=side):
                 halo_copy(side).wait_recv()
 
-        @pl.loop(0, slots - n)
-        def _(k):
-            before = idx[o_dprev + k]
-
-            def write(at, y):
-                acc[n + k, :, at] = acc[before, :, at] + y
-
-            product(ext[idx[o_dcol + k]], idx[o_dord + k], 1, write)
-
-        for b in block_order(n):
-            snd[b] = acc[idx[o_dlast + b]].astype(jnp.bfloat16).reshape(snd.shape[1:])
+        def slot(k):
+            product(ext[idx[o_dcol + k]], idx[o_dord + k], 1, keep(n + k))
+
+        def send(p):
+            b = down_block(p, n)
+            total = acc[b]
+            for d in range(SPAN):
+                if d != BAND:
+                    total = total + acc[idx[o_dat + b * SPAN + d]]
+            snd[b] = total.astype(jnp.bfloat16).reshape(snd.shape[1:])
             fwd_copy(b).start()
 
-    for b in range(n):
+        chunked(slots - n, slot, send)
+        pl.loop((slots - n) // CHUNK, n)(send)
+
+    early = max(0, n - BAND - n // 2)
+
+    def up_arrival(p):
+        b = up_block(p, n)
+
         @pl.when(has_next)
-        def _(b=b):
+        def _():
             bwd_copy(b).wait_recv()
             total = ext[BAND + b].astype(jnp.float32) + binc[b].astype(jnp.float32)
             up[b] = total.astype(jnp.bfloat16)
 
         @pl.when(jnp.logical_not(has_next))
-        def _(b=b):
+        def _():
             up[b] = ext[BAND + b]
 
         up_copy(b).start()
 
+        @pl.when(has_prev)
+        def _():
+            product(up[b], idx[o_table + b * SPAN + BAND], 0, keep(b))
+
+    pl.loop(0, early + border)(up_arrival)
+
     @pl.when(has_prev)
     def _():
-        acc[slots] = jnp.zeros(acc.shape[1:], acc.dtype)
-
-        def slot(k):
-            before = idx[o_uprev + k]
-
-            def write(at, y):
-                acc[k, :, at] = acc[before, :, at] + y
-
-            product(up[idx[o_urow + k]], idx[o_uord + k], 0, write)
-
-        rims = min(slots, BAND * (BAND + 1))
-        pl.loop(0, rims)(slot)
+        @pl.loop(0, RIMS // 2)
+        def _(j):
+            low, high = j // 2, n - BAND + (j + 1) // 2
+            product(up[low], idx[o_table + low * SPAN + j % 2], 0, keep(n + j))
+            product(
+                up[high], idx[o_table + high * SPAN + SPAN - 1 - j % 2], 0,
+                keep(n + RIMS // 2 + j),
+            )
+
         for side, there in enumerate((has_left, has_right)):
             for b in range(BAND):
-                c = b if side == 0 else BAND + n + b
-                rim_snd[side, b] = (
-                    acc[idx[o_ulast + c]].astype(jnp.bfloat16).reshape(rim_snd.shape[2:])
-                )
+                c = b - BAND if side == 0 else n + b
+                near = [r for r in range(n) if abs(c - r) <= BAND]
+                total = sum(acc[idx[o_uat + r * SPAN + c - r + BAND]] for r in near)
+                rim_snd[side, b] = total.astype(jnp.bfloat16).reshape(rim_snd.shape[2:])
 
             @pl.when(there)
             def _(side=side):
                 rim_copy(side).start()
-        pl.loop(rims, slots)(slot)
-        inside = [b for b in range(n) if BAND <= b < n - BAND]
-        border = [b for b in range(n) if b not in inside]
-        for b in inside:
-            bsnd[b] = acc[idx[o_ulast + BAND + b]].astype(jnp.bfloat16).reshape(bsnd.shape[1:])
+
+    pl.loop(early + border, n)(up_arrival)
+
+    @pl.when(has_prev)
+    def _():
+        def slot(k):
+            product(up[idx[o_urow + k]], idx[o_uord + k], 0, keep(n + RIMS + k))
+
+        def summed(b):
+            total = acc[b]
+            for r in range(-BAND, SPAN - BAND):
+                if r != 0:
+                    at = (b + r) * SPAN - r + BAND
+                    inside = (b + r >= 0) & (b + r < n)
+                    place = idx[o_uat + jnp.clip(at, 0, n * SPAN - 1)]
+                    total = total + acc[jnp.where(inside, place, zero)]
+            return total.reshape(bsnd.shape[1:])
+
+        def send_inside(p):
+            b = up_block(p, n)
+            bsnd[b] = summed(b).astype(jnp.bfloat16)
             bwd_copy(b).start()
+
+        def after(p):
+            @pl.when(p < early)
+            def _():
+                send_inside(p)
+
+        chunked(rest, slot, after)
+        pl.loop(min(early, rest // CHUNK), early)(send_inside)
         for side, there in enumerate((has_right, has_left)):
             @pl.when(there)
             def _(side=side):
                 rim_copy(side).wait_recv()
-        for b in border:
-            total = acc[idx[o_ulast + BAND + b]].reshape(bsnd.shape[1:])
+        for p in range(early, early + border):
+            b = up_block(p, n)
+            total = summed(b)
             if b < BAND:
                 total = total + rim_rcv[1, b].astype(jnp.float32)
             if b >= n - BAND:
                 total = total + rim_rcv[0, b - (n - BAND)].astype(jnp.float32)
             bsnd[b] = total.astype(jnp.bfloat16)
             bwd_copy(b).start()
+        pl.loop(early + border, n)(send_inside)
 
     for b in range(n):
         down_copy(b).wait()
@@ -311,13 +364,15 @@
     slots, tile = tile_data.shape[1], tile_data.shape[3]
     _, parts, half, length = source.shape
     n = length // tile
-    idx, offsets = plan(tile_rows[0], tile_cols[0], tile_count[0, 0], lax.axis_index("blk") * n, n)
+    rest = slots - n - min(1, groups - 1)
+    first_block = lax.axis_index("blk") * n
+    idx, offsets = plan(tile_rows[0], tile_cols[0], tile_count[0, 0], first_block, n, rest)
     block = (parts, half, tile)
     bf16 = jnp.bfloat16
     dma = pltpu.SemaphoreType.DMA
     shape = jax.ShapeDtypeStruct((parts, half, length), bf16)
     down, up = pl.pallas_call(
-        functools.partial(kernel, layers, groups, n, slots, offsets),
+        functools.partial(kernel, layers, groups, n, slots, rest, offsets),
         out_shape=(shape, shape),
         in_specs=[
             pl.BlockSpec(memory_space=pltpu.SMEM),
@@ -327,7 +382,7 @@
         out_specs=(pl.BlockSpec(memory_space=pl.ANY), pl.BlockSpec(memory_space=pl.ANY)),
         scratch_shapes=[
             pltpu.VMEM((slots, 2, tile, tile), bf16),
-            pltpu.VMEM((slots + 1, parts * half, tile), jnp.float32),
+            pltpu.VMEM((max(slots, n + RIMS + rest) + 1, parts * half, tile), jnp.float32),
             pltpu.VMEM((n,) + block, bf16),
             pltpu.VMEM((n + 2 * BAND,) + block, bf16),
             pltpu.VMEM((n,) + block, bf16),

time: 172 us -> 155 us (0.901)
  Pallas kernels: 163 us -> 146 us
    pallas_call x1, Pallas kernels: 163 us -> 146 us  [on_device(): pl.pallas_call(functools.partial(kernel, layers, groups, n, slots, rest,...]
where the time goes in v2:
time: 155 us
  Pallas kernels  146 us (94%)
  local copies, waits for them, and re-layouts  5.28 us (3%)
  other arithmetic  2 us (1%)
    pallas_call x1, Pallas kernels, on_device(): pl.pallas_call(functools.partial(kernel, layers, groups, n, slots, rest,...  146 us
    unnamed x4, local copies, waits for them, and re-layouts  4.6 us

profile of v2, /device:TPU:16, one launch (start us, length us, event | category | flops | bytes accessed | tf_op | source)
XLA Modules:
  0.0 154.7 jit_solution(7611997319606498317)
XLA Ops:
  1.3 0.7 broadcast_add_fusion
  2.0 0.7 fusion.21
  2.7 0.2 convert_reduce_fusion
  2.9 0.1 fusion
  3.0 0.1 select_reduce_fusion
  3.1 0.1 select_reduce_fusion.1
  3.2 0.1 select_reduce_fusion.2
  3.4 0.7 concatenate.3.idx
  4.0 146.1 %shard_map.68 = (bf16[2,128,4096]{2,1,0:T(8,128)(2,1)}, bf16[2,128,4096]{2,1,0:T(8,128)(2,1)}) custom-call(s32[216]{0:T(256)} %concatenate.3.idx, bf16[2,128,4096]{2,1,0:T(8,128)(2,1)} %bitcast.68, bf16[24,2,512,512]{3,2,1,0:T(8,128)(2,1)} %bitcast.65), custom_call_target="tpu_custom_call" | custom-call | tf_op jit(solution)/shard_map/pallas_call | solution.py:374
  150.1 0.0 copy-start
  150.1 3.3 %copy.10 = bf16[1,2,128,4096]{3,2,1,0:T(8,128)(2,1)} copy(bf16[1,2,128,4096]{3,2,1,0:T(8,128)(2,1)} %bitcast.67) | data formatting | bytes 4194304
  153.4 0.0 copy-done
  153.4 1.3 copy.11
  (13 shorter events, 0.1 us)
Async XLA Ops:
  150.1 3.3 %copy-start = (bf16[2,128,4096]{2,1,0:T(8,128)(2,1)S(1)}, bf16[2,128,4096]{2,1,0:T(8,128)(2,1)}, u32[]{:S(2)}) copy-start(bf16[2,128,4096]{2,1,0:T(8,128)(2,1)} %get-tuple-element.5) | copy-start | bytes 6291460

commit v3 on v2

--- a/solution.py
+++ b/solution.py
@@ -111,20 +111,18 @@
             recv_sem=binc_recv.at[b], device_id=to_prev, device_id_type=MESH,
         )
 
-    def halo_copy(side):
-        if side == 0:
-            a, b, dev = ext.at[pl.ds(BAND, BAND)], ext.at[pl.ds(BAND + n, BAND)], to_left
-        else:
-            a, b, dev = ext.at[pl.ds(n, BAND)], ext.at[pl.ds(0, BAND)], to_right
+    def halo_copy(side, i):
+        near, far, dev = (BAND + i, BAND + n + i, to_left) if side == 0 else (n + i, i, to_right)
         return pltpu.make_async_remote_copy(
-            src_ref=a, dst_ref=b, send_sem=halo_send.at[side],
-            recv_sem=halo_recv.at[side], device_id=dev, device_id_type=MESH,
-        )
-
-    def rim_copy(side):
+            src_ref=ext.at[near], dst_ref=ext.at[far], send_sem=halo_send.at[side, i],
+            recv_sem=halo_recv.at[side, i], device_id=dev, device_id_type=MESH,
+        )
+
+    def rim_copy(side, i):
         return pltpu.make_async_remote_copy(
-            src_ref=rim_snd.at[side], dst_ref=rim_rcv.at[side], send_sem=rim_send.at[side],
-            recv_sem=rim_recv.at[side], device_id=(to_left, to_right)[side], device_id_type=MESH,
+            src_ref=rim_snd.at[side, i], dst_ref=rim_rcv.at[side, i],
+            send_sem=rim_send.at[side, i], recv_sem=rim_recv.at[side, i],
+            device_id=(to_left, to_right)[side], device_id_type=MESH,
         )
 
     for p in range(n):
@@ -142,18 +140,16 @@
     pl.semaphore_wait(barrier, sum(there.astype(jnp.int32) for there, _ in partners))
 
     def product(x, s, dim, write):
-        x1 = x.reshape(2 * half, tile)
-        x2 = jnp.concatenate([-x[1], x[0]], axis=0)
+        both = jnp.concatenate(
+            [x.reshape(2 * half, tile), jnp.concatenate([-x[1], x[0]], axis=0)], axis=1
+        )
+        if dim == 1:
+            matrix = jnp.concatenate([tiles[s, 0], tiles[s, 1]], axis=1)
+        else:
+            matrix = tiles[s].reshape(2 * tile, tile)
         numbers = (((1,), (dim,)), ((), ()))
-        step = min(tile, 256)
-        for j in range(0, tile, step):
-            if dim == 1:
-                real, imag = tiles[s, 0, j:j + step, :], tiles[s, 1, j:j + step, :]
-            else:
-                real, imag = tiles[s, 0, :, j:j + step], tiles[s, 1, :, j:j + step]
-            y = lax.dot_general(x1, real, numbers, preferred_element_type=jnp.float32)
-            y = y + lax.dot_general(x2, imag, numbers, preferred_element_type=jnp.float32)
-            write(slice(j, j + step), y)
+        y = lax.dot_general(both, matrix, numbers, preferred_element_type=jnp.float32)
+        write(slice(None), y)
 
     @pl.when(jnp.logical_not(has_left))
     def _():
@@ -183,38 +179,45 @@
         for k in range(total // CHUNK * CHUNK, total):
             slot(k)
 
+    border = min(n, 2 * BAND)
+
+    def down_arrival(p):
+        b = down_block(p, n)
+        src_copy(b).wait()
+
+        @pl.when(has_prev)
+        def _():
+            fwd_copy(b).wait_recv()
+            total = src[b].astype(jnp.float32) + inc[b].astype(jnp.float32)
+            ext[BAND + b] = total.astype(jnp.bfloat16)
+
+        @pl.when(jnp.logical_not(has_prev))
+        def _():
+            ext[BAND + b] = src[b]
+
+        down_copy(b).start()
+
+    def down_diagonal(p):
+        b = down_block(p, n)
+        product(ext[BAND + b], idx[o_table + b * SPAN + BAND], 1, keep(b))
+
+    @pl.loop(0, border)
+    def _(p):
+        b = down_block(p, n)
+        down_arrival(p)
+
+        @pl.when(has_next & has_right & (b >= n - BAND))
+        def _():
+            halo_copy(1, b - (n - BAND)).start()
+
+        @pl.when(has_next & has_left & (b < BAND))
+        def _():
+            halo_copy(0, b).start()
+
     @pl.loop(0, slots)
     def _(s):
         tile_copy(s).wait()
 
-    border = min(n, 2 * BAND)
-
-    def down_arrival(p):
-        b = down_block(p, n)
-        src_copy(b).wait()
-
-        @pl.when(has_prev)
-        def _():
-            fwd_copy(b).wait_recv()
-            total = src[b].astype(jnp.float32) + inc[b].astype(jnp.float32)
-            ext[BAND + b] = total.astype(jnp.bfloat16)
-
-        @pl.when(jnp.logical_not(has_prev))
-        def _():
-            ext[BAND + b] = src[b]
-
-        down_copy(b).start()
-
-    def down_diagonal(p):
-        b = down_block(p, n)
-        product(ext[BAND + b], idx[o_table + b * SPAN + BAND], 1, keep(b))
-
-    pl.loop(0, border)(down_arrival)
-    for side, there in enumerate((has_left, has_right)):
-        @pl.when(has_next & there)
-        def _(side=side):
-            halo_copy(side).start()
-
     @pl.when(has_next)
     def _():
         pl.loop(0, border)(down_diagonal)
@@ -232,7 +235,8 @@
         for side, there in enumerate((has_right, has_left)):
             @pl.when(there)
             def _(side=side):
-                halo_copy(side).wait_recv()
+                for i in range(BAND):
+                    halo_copy(side, i).wait_recv()
 
         def slot(k):
             product(ext[idx[o_dcol + k]], idx[o_dord + k], 1, keep(n + k))
@@ -251,6 +255,9 @@
 
     early = max(0, n - BAND - n // 2)
 
+    def up_diagonal(b):
+        product(up[b], idx[o_table + b * SPAN + BAND], 0, keep(b))
+
     def up_arrival(p):
         b = up_block(p, n)
 
@@ -266,35 +273,44 @@
 
         up_copy(b).start()
 
-        @pl.when(has_prev)
-        def _():
-            product(up[b], idx[o_table + b * SPAN + BAND], 0, keep(b))
+        @pl.when(has_prev & has_next)
+        def _():
+            up_diagonal(b)
 
     pl.loop(0, early + border)(up_arrival)
 
     @pl.when(has_prev)
     def _():
-        @pl.loop(0, RIMS // 2)
-        def _(j):
-            low, high = j // 2, n - BAND + (j + 1) // 2
+        def rim_pair(j):
+            low, high = j // 2, n - BAND + (BAND + 1 - j) // 2
             product(up[low], idx[o_table + low * SPAN + j % 2], 0, keep(n + j))
             product(
                 up[high], idx[o_table + high * SPAN + SPAN - 1 - j % 2], 0,
-                keep(n + RIMS // 2 + j),
+                keep(n + RIMS - 1 - j),
             )
 
-        for side, there in enumerate((has_left, has_right)):
-            for b in range(BAND):
-                c = b - BAND if side == 0 else n + b
-                near = [r for r in range(n) if abs(c - r) <= BAND]
-                total = sum(acc[idx[o_uat + r * SPAN + c - r + BAND]] for r in near)
-                rim_snd[side, b] = total.astype(jnp.bfloat16).reshape(rim_snd.shape[2:])
-
-            @pl.when(there)
-            def _(side=side):
-                rim_copy(side).start()
+        def rim_start(side, b):
+            c = b - BAND if side == 0 else n + b
+            near = [r for r in range(n) if abs(c - r) <= BAND]
+            total = sum(acc[idx[o_uat + r * SPAN + c - r + BAND]] for r in near)
+            rim_snd[side, b] = total.astype(jnp.bfloat16).reshape(rim_snd.shape[2:])
+
+            @pl.when((has_left, has_right)[side])
+            def _():
+                rim_copy(side, b).start()
+
+        rim_pair(0)
+        rim_start(0, 0)
+        rim_start(1, 1)
+        pl.loop(1, RIMS // 2)(rim_pair)
+        rim_start(0, 1)
+        rim_start(1, 0)
 
     pl.loop(early + border, n)(up_arrival)
+
+    @pl.when(has_prev & jnp.logical_not(has_next))
+    def _():
+        pl.loop(0, n)(up_diagonal)
 
     @pl.when(has_prev)
     def _():
@@ -326,7 +342,8 @@
         for side, there in enumerate((has_right, has_left)):
             @pl.when(there)
             def _(side=side):
-                rim_copy(side).wait_recv()
+                for i in range(BAND):
+                    rim_copy(side, i).wait_recv()
         for p in range(early, early + border):
             b = up_block(p, n)
             total = summed(b)
@@ -352,11 +369,13 @@
     for side, there in enumerate((has_left, has_right)):
         @pl.when(has_next & there)
         def _(side=side):
-            halo_copy(side).wait_send()
+            for i in range(BAND):
+                halo_copy(side, i).wait_send()
 
         @pl.when(has_prev & there)
         def _(side=side):
-            rim_copy(side).wait_send()
+            for i in range(BAND):
+                rim_copy(side, i).wait_send()
 
 
 def on_device(source, tile_data, tile_rows, tile_cols, tile_count):
@@ -399,10 +418,10 @@
             dma((n,)),
             dma((n,)),
             dma((n,)),
-            dma((2,)),
-            dma((2,)),
-            dma((2,)),
-            dma((2,)),
+            dma((2, BAND)),
+            dma((2, BAND)),
+            dma((2, BAND)),
+            dma((2, BAND)),
         ],
         compiler_params=pltpu.CompilerParams(
             collective_id=0, has_side_effects=True, vmem_limit_bytes=62 * 1024 * 1024

time: 155 us -> 139 us (0.90)
  Pallas kernels: 146 us -> 130 us
    pallas_call x1, Pallas kernels: 146 us -> 130 us  [on_device(): pl.pallas_call(functools.partial(kernel, layers, groups, n, slots, rest,...]
where the time goes in v3:
time: 139 us
  Pallas kernels  130 us (94%)
  local copies, waits for them, and re-layouts  5.28 us (4%)
  other arithmetic  2 us (1%)
    pallas_call x1, Pallas kernels, on_device(): pl.pallas_call(functools.partial(kernel, layers, groups, n, slots, rest,...  130 us
    unnamed x4, local copies, waits for them, and re-layouts  4.6 us

profile of v3, /device:TPU:16, one launch (start us, length us, event | category | flops | bytes accessed | tf_op | source)
XLA Modules:
  0.0 138.5 jit_solution(6191383436673262690)
XLA Ops:
  1.3 0.7 broadcast_add_fusion
  2.0 0.7 fusion.21
  2.7 0.2 convert_reduce_fusion
  2.9 0.1 fusion
  3.0 0.1 select_reduce_fusion
  3.1 0.1 select_reduce_fusion.1
  3.2 0.1 select_reduce_fusion.2
  3.4 0.7 concatenate.3.idx
  4.0 129.9 %shard_map.68 = (bf16[2,128,4096]{2,1,0:T(8,128)(2,1)}, bf16[2,128,4096]{2,1,0:T(8,128)(2,1)}) custom-call(s32[216]{0:T(256)} %concatenate.3.idx, bf16[2,128,4096]{2,1,0:T(8,128)(2,1)} %bitcast.68, bf16[24,2,512,512]{3,2,1,0:T(8,128)(2,1)} %bitcast.65), custom_call_target="tpu_custom_call" | custom-call | tf_op jit(solution)/shard_map/pallas_call | solution.py:393
  133.9 0.0 copy-start
  133.9 3.3 %copy.10 = bf16[1,2,128,4096]{3,2,1,0:T(8,128)(2,1)} copy(bf16[1,2,128,4096]{3,2,1,0:T(8,128)(2,1)} %bitcast.67) | data formatting | bytes 4194304
  137.2 0.0 copy-done
  137.2 1.3 copy.11
  (13 shorter events, 0.1 us)
Async XLA Ops:
  133.9 3.3 %copy-start = (bf16[2,128,4096]{2,1,0:T(8,128)(2,1)S(1)}, bf16[2,128,4096]{2,1,0:T(8,128)(2,1)}, u32[]{:S(2)}) copy-start(bf16[2,128,4096]{2,1,0:T(8,128)(2,1)} %get-tuple-element.5) | copy-start | bytes 6291460

commit v4 on v3

--- a/solution.py
+++ b/solution.py
@@ -20,8 +20,12 @@
     return (p + n - BAND) % n
 
 
+def up_early(n):
+    return max(0, n - 2 * BAND - 1)
+
+
 def up_block(p, n):
-    return (p + n // 2) % n
+    return (p + n - BAND - up_early(n)) % n
 
 
 def sorted_by(key, values):
@@ -45,7 +49,7 @@
     key = jnp.where(diag, key + 2 * big, key)
     rank, (d_ord, d_col) = sorted_by(key, jnp.stack([ids, c + BAND]))
     d_pos = jnp.where(diag, r, n + rank)
-    key = jnp.where(live, ((c + n - n // 2) % n) * slots, big) + ids
+    key = jnp.where(live, ((c + BAND + up_early(n)) % n) * slots, big) + ids
     key = jnp.where(diag | rim, key + 2 * big, key)
     rank, (u_ord, u_row) = sorted_by(key, jnp.stack([ids, r]))
     rim_at = jnp.where(left, r + c + BAND, RIMS // 2 + r + BAND - n + c - n)
@@ -169,8 +173,8 @@
 
         return write
 
-    def chunked(total, slot, after):
-        @pl.loop(0, total // CHUNK)
+    def chunked(total, slot, after, first=0):
+        @pl.loop(first, total // CHUNK)
         def _(p):
             for j in range(CHUNK):
                 slot(p * CHUNK + j)
@@ -253,7 +257,7 @@
         chunked(slots - n, slot, send)
         pl.loop((slots - n) // CHUNK, n)(send)
 
-    early = max(0, n - BAND - n // 2)
+    early = up_early(n)
 
     def up_diagonal(b):
         product(up[b], idx[o_table + b * SPAN + BAND], 0, keep(b))
@@ -279,33 +283,29 @@
 
     pl.loop(0, early + border)(up_arrival)
 
+    def rim_pair(j):
+        low, high = j // 2, n - BAND + (BAND + 1 - j) // 2
+        product(up[low], idx[o_table + low * SPAN + j % 2], 0, keep(n + j))
+        product(
+            up[high], idx[o_table + high * SPAN + SPAN - 1 - j % 2], 0,
+            keep(n + RIMS - 1 - j),
+        )
+
+    def rim_start(side, b):
+        c = b - BAND if side == 0 else n + b
+        near = [r for r in range(n) if abs(c - r) <= BAND]
+        total = sum(acc[idx[o_uat + r * SPAN + c - r + BAND]] for r in near)
+        rim_snd[side, b] = total.astype(jnp.bfloat16).reshape(rim_snd.shape[2:])
+
+        @pl.when((has_left, has_right)[side])
+        def _():
+            rim_copy(side, b).start()
+
     @pl.when(has_prev)
     def _():
-        def rim_pair(j):
-            low, high = j // 2, n - BAND + (BAND + 1 - j) // 2
-            product(up[low], idx[o_table + low * SPAN + j % 2], 0, keep(n + j))
-            product(
-                up[high], idx[o_table + high * SPAN + SPAN - 1 - j % 2], 0,
-                keep(n + RIMS - 1 - j),
-            )
-
-        def rim_start(side, b):
-            c = b - BAND if side == 0 else n + b
-            near = [r for r in range(n) if abs(c - r) <= BAND]
-            total = sum(acc[idx[o_uat + r * SPAN + c - r + BAND]] for r in near)
-            rim_snd[side, b] = total.astype(jnp.bfloat16).reshape(rim_snd.shape[2:])
-
-            @pl.when((has_left, has_right)[side])
-            def _():
-                rim_copy(side, b).start()
-
         rim_pair(0)
         rim_start(0, 0)
         rim_start(1, 1)
-        pl.loop(1, RIMS // 2)(rim_pair)
-        rim_start(0, 1)
-        rim_start(1, 0)
-
     pl.loop(early + border, n)(up_arrival)
 
     @pl.when(has_prev & jnp.logical_not(has_next))
@@ -337,7 +337,15 @@
             def _():
                 send_inside(p)
 
-        chunked(rest, slot, after)
+        first = min(1, rest // CHUNK)
+        for k in range(first * CHUNK):
+            slot(k)
+        if first and early:
+            send_inside(0)
+        pl.loop(1, RIMS // 2)(rim_pair)
+        rim_start(0, 1)
+        rim_start(1, 0)
+        chunked(rest, slot, after, first)
         pl.loop(min(early, rest // CHUNK), early)(send_inside)
         for side, there in enumerate((has_right, has_left)):
             @pl.when(there)
@@ -376,6 +384,18 @@
         def _(side=side):
             for i in range(BAND):
                 rim_copy(side, i).wait_send()
+
+
+def hand_out(down_in, up_in, down_out, up_out, sem):
+    copies = [
+        pltpu.make_async_copy(a.at[h], b.at[h], sem.at[i, h])
+        for i, (a, b) in enumerate(((down_in, down_out), (up_in, up_out)))
+        for h in range(2)
+    ]
+    for copy in copies:
+        copy.start()
+    for copy in copies:
+        copy.wait()
 
 
 def on_device(source, tile_data, tile_rows, tile_cols, tile_count):
@@ -427,6 +447,14 @@
             collective_id=0, has_side_effects=True, vmem_limit_bytes=62 * 1024 * 1024
         ),
     )(idx, source[0], tile_data[0])
+    down, up = pl.pallas_call(
+        hand_out,
+        out_shape=(shape, shape),
+        in_specs=[pl.BlockSpec(memory_space=pl.ANY)] * 2,
+        out_specs=(pl.BlockSpec(memory_space=pl.ANY),) * 2,
+        scratch_shapes=[dma((2, 2))],
+        compiler_params=pltpu.CompilerParams(vmem_limit_bytes=62 * 1024 * 1024),
+    )(down, up)
     return (down[None], up[None])
 
 

time: 139 us -> 263 us (1.89)
  Pallas kernels: 130 us -> 259 us
  local copies, waits for them, and re-layouts: 5.28 us -> 0.68 us
    pallas_call x0 -> x1, Pallas kernels: none -> 128 us  [on_device(): pl.pallas_call(hand_out, out_shape=(shape, shape), in_specs=[pl.BlockSpec...]
    unnamed x4 -> x0, local copies, waits for them, and re-layouts: 4.6 us -> none
where the time goes in v4:
time: 263 us
  Pallas kernels  259 us (98%)
    pallas_call x1, Pallas kernels, on_device(): pl.pallas_call(functools.partial(kernel, layers, groups, n, slots, rest,...  131 us
    pallas_call x1, Pallas kernels, on_device(): pl.pallas_call(hand_out, out_shape=(shape, shape), in_specs=[pl.BlockSpec...  128 us

profile of v4, /device:TPU:16, one launch (start us, length us, event | category | flops | bytes accessed | tf_op | source)
XLA Modules:
  0.0 263.1 jit_solution(6600298419453315529)
XLA Ops:
  1.3 0.7 broadcast_add_fusion
  2.0 0.7 fusion.21
  2.7 0.2 convert_reduce_fusion
  2.9 0.1 fusion
  3.0 0.1 select_reduce_fusion
  3.1 0.1 select_reduce_fusion.1
  3.2 0.1 select_reduce_fusion.2
  3.4 0.7 concatenate.3.idx
  4.0 130.9 %shard_map.68 = (bf16[2,128,4096]{2,1,0:T(8,128)(2,1)}, bf16[2,128,4096]{2,1,0:T(8,128)(2,1)}) custom-call(s32[216]{0:T(256)} %concatenate.3.idx, bf16[2,128,4096]{2,1,0:T(8,128)(2,1)} %bitcast.66, bf16[24,2,512,512]{3,2,1,0:T(8,128)(2,1)} %bitcast.65), custom_call_target="tpu_custom_call" | custom-call | tf_op jit(solution)/shard_map/pallas_call | solution.py:413
  134.9 128.2 %shard_map.69 = (bf16[2,128,4096]{2,1,0:T(8,128)(2,1)}, bf16[2,128,4096]{2,1,0:T(8,128)(2,1)}) custom-call(bf16[2,128,4096]{2,1,0:T(8,128)(2,1)} %get-tuple-element.6.down_in, bf16[2,128,4096]{2,1,0:T(8,128)(2,1)} %get-tuple-element.7.up_in), custom_call_target="tpu_custom_call" | custom-call | tf_op jit(solution)/shard_map/pallas_call | solution.py:450
  (13 shorter events, 0.1 us)

commit v5 on v4

--- a/solution.py
+++ b/solution.py
@@ -301,11 +301,23 @@
         def _():
             rim_copy(side, b).start()
 
+    def later_rims():
+        pl.loop(1, RIMS // 2)(rim_pair)
+        rim_start(0, 1)
+        rim_start(1, 0)
+
+    rims_first = layer % 2 == 1
+
     @pl.when(has_prev)
     def _():
         rim_pair(0)
         rim_start(0, 0)
         rim_start(1, 1)
+
+        @pl.when(rims_first)
+        def _():
+            later_rims()
+
     pl.loop(early + border, n)(up_arrival)
 
     @pl.when(has_prev & jnp.logical_not(has_next))
@@ -342,9 +354,11 @@
             slot(k)
         if first and early:
             send_inside(0)
-        pl.loop(1, RIMS // 2)(rim_pair)
-        rim_start(0, 1)
-        rim_start(1, 0)
+
+        @pl.when(jnp.logical_not(rims_first))
+        def _():
+            later_rims()
+
         chunked(rest, slot, after, first)
         pl.loop(min(early, rest // CHUNK), early)(send_inside)
         for side, there in enumerate((has_right, has_left)):
@@ -384,18 +398,6 @@
         def _(side=side):
             for i in range(BAND):
                 rim_copy(side, i).wait_send()
-
-
-def hand_out(down_in, up_in, down_out, up_out, sem):
-    copies = [
-        pltpu.make_async_copy(a.at[h], b.at[h], sem.at[i, h])
-        for i, (a, b) in enumerate(((down_in, down_out), (up_in, up_out)))
-        for h in range(2)
-    ]
-    for copy in copies:
-        copy.start()
-    for copy in copies:
-        copy.wait()
 
 
 def on_device(source, tile_data, tile_rows, tile_cols, tile_count):
@@ -447,14 +449,6 @@
             collective_id=0, has_side_effects=True, vmem_limit_bytes=62 * 1024 * 1024
         ),
     )(idx, source[0], tile_data[0])
-    down, up = pl.pallas_call(
-        hand_out,
-        out_shape=(shape, shape),
-        in_specs=[pl.BlockSpec(memory_space=pl.ANY)] * 2,
-        out_specs=(pl.BlockSpec(memory_space=pl.ANY),) * 2,
-        scratch_shapes=[dma((2, 2))],
-        compiler_params=pltpu.CompilerParams(vmem_limit_bytes=62 * 1024 * 1024),
-    )(down, up)
     return (down[None], up[None])
 
 

time: 263 us -> 139 us (0.53)
  Pallas kernels: 259 us -> 130 us
  local copies, waits for them, and re-layouts: 0.68 us -> 5.28 us
    pallas_call x1 -> x0, Pallas kernels: 128 us -> none  [on_device(): pl.pallas_call(hand_out, out_shape=(shape, shape), in_specs=[pl.BlockSpec...]
    unnamed x0 -> x4, local copies, waits for them, and re-layouts: none -> 4.6 us
where the time goes in v5:
time: 139 us; the launch traced here: 138 us
  Pallas kernels  130 us (94%)
  local copies, waits for them, and re-layouts  5.28 us (4%)
  other arithmetic  2 us (1%)
    pallas_call x1, Pallas kernels, on_device(): pl.pallas_call(functools.partial(kernel, layers, groups, n, slots, rest,...  130 us
    unnamed x4, local copies, waits for them, and re-layouts  4.6 us

profile of v5, /device:TPU:16, one launch (start us, length us, event | category | flops | bytes accessed | tf_op | source)
XLA Modules:
  0.0 138.3 jit_solution(13315175531528518109)
XLA Ops:
  1.3 0.7 broadcast_add_fusion
  2.0 0.7 fusion.21
  2.7 0.2 convert_reduce_fusion
  2.9 0.1 fusion
  3.0 0.1 select_reduce_fusion
  3.1 0.1 select_reduce_fusion.1
  3.2 0.1 select_reduce_fusion.2
  3.4 0.7 concatenate.3.idx
  4.0 129.7 %shard_map.68 = (bf16[2,128,4096]{2,1,0:T(8,128)(2,1)}, bf16[2,128,4096]{2,1,0:T(8,128)(2,1)}) custom-call(s32[216]{0:T(256)} %concatenate.3.idx, bf16[2,128,4096]{2,1,0:T(8,128)(2,1)} %bitcast.68, bf16[24,2,512,512]{3,2,1,0:T(8,128)(2,1)} %bitcast.65), custom_call_target="tpu_custom_call" | custom-call | tf_op jit(solution)/shard_map/pallas_call | solution.py:415
  133.7 0.0 copy-start
  133.7 3.3 %copy.10 = bf16[1,2,128,4096]{3,2,1,0:T(8,128)(2,1)} copy(bf16[1,2,128,4096]{3,2,1,0:T(8,128)(2,1)} %bitcast.67) | data formatting | bytes 4194304
  137.0 0.0 copy-done
  137.0 1.3 copy.11
  (13 shorter events, 0.1 us)
Async XLA Ops:
  133.7 3.3 %copy-start = (bf16[2,128,4096]{2,1,0:T(8,128)(2,1)S(1)}, bf16[2,128,4096]{2,1,0:T(8,128)(2,1)}, u32[]{:S(2)}) copy-start(bf16[2,128,4096]{2,1,0:T(8,128)(2,1)} %get-tuple-element.5) | copy-start | bytes 6291460

commit v6 on v5

--- a/solution.py
+++ b/solution.py
@@ -21,7 +21,7 @@
 
 
 def up_early(n):
-    return max(0, n - 2 * BAND - 1)
+    return max(0, (n - 2 * BAND) // 2)
 
 
 def up_block(p, n):

time: 139 us -> 139 us (level)
  no operation moved by 1% of the time
where the time goes in v6:
time: 139 us
  Pallas kernels  130 us (94%)
  local copies, waits for them, and re-layouts  5.28 us (4%)
  other arithmetic  2 us (1%)
    pallas_call x1, Pallas kernels, on_device(): pl.pallas_call(functools.partial(kernel, layers, groups, n, slots, rest,...  130 us
    unnamed x4, local copies, waits for them, and re-layouts  4.6 us

profile of v6, /device:TPU:16, one launch (start us, length us, event | category | flops | bytes accessed | tf_op | source)
XLA Modules:
  0.0 138.6 jit_solution(12831619248242972381)
XLA Ops:
  1.3 0.7 broadcast_add_fusion
  2.0 0.7 fusion.21
  2.7 0.2 convert_reduce_fusion
  2.9 0.1 fusion
  3.0 0.1 select_reduce_fusion
  3.1 0.1 select_reduce_fusion.1
  3.2 0.1 select_reduce_fusion.2
  3.4 0.7 concatenate.3.idx
  4.0 129.9 %shard_map.68 = (bf16[2,128,4096]{2,1,0:T(8,128)(2,1)}, bf16[2,128,4096]{2,1,0:T(8,128)(2,1)}) custom-call(s32[216]{0:T(256)} %concatenate.3.idx, bf16[2,128,4096]{2,1,0:T(8,128)(2,1)} %bitcast.68, bf16[24,2,512,512]{3,2,1,0:T(8,128)(2,1)} %bitcast.65), custom_call_target="tpu_custom_call" | custom-call | tf_op jit(solution)/shard_map/pallas_call | solution.py:415
  134.0 0.0 copy-start
  134.0 3.3 %copy.10 = bf16[1,2,128,4096]{3,2,1,0:T(8,128)(2,1)} copy(bf16[1,2,128,4096]{3,2,1,0:T(8,128)(2,1)} %bitcast.67) | data formatting | bytes 4194304
  137.3 0.0 copy-done
  137.3 1.3 copy.11
  (13 shorter events, 0.1 us)
Async XLA Ops:
  134.0 3.3 %copy-start = (bf16[2,128,4096]{2,1,0:T(8,128)(2,1)S(1)}, bf16[2,128,4096]{2,1,0:T(8,128)(2,1)}, u32[]{:S(2)}) copy-start(bf16[2,128,4096]{2,1,0:T(8,128)(2,1)} %get-tuple-element.5) | copy-start | bytes 6291460
